TPU v7x, 128 devices: a whole 4x4x4 slice. The times are simulated.
128 devices in a mesh: group: 4 (over y), dom: 32 (over z, x, core).
Axes of the slice: x: 4, y: 4, z: 4, core: 2. Of those that a mesh axis runs over, the one named last changes fastest.
Arguments:
- nodes: bfloat16 [262144, 128], P(('group', 'dom')), may hold values from -6 to 6
- mesh_edges: bfloat16 [1572864, 128], P(('group', 'dom')), may hold values from -6 to 6
- contact_edges: bfloat16 [16384, 64, 128], P(('group', 'dom')), may hold values from -6 to 6
- mesh_src: int32 [1572864], P(('group', 'dom')), may hold values from 0 to 2559, as said below
- halo_rows: int32 [256, 256], P(('group', 'dom')), may hold values from 0 to 2047
- send_rows: int32 [16384, 64], P(('group', 'dom')), may hold values from 0 to 2047
- partner_rows: int32 [16384, 64], P(('group', 'dom')), may hold values from 0 to 2047
- contact_counts: int32 [128, 128], replicated, may hold values from 1 to 64, as said below
- edge_first: bfloat16 [384, 128], replicated, may hold values from -0.3125 to 0.3125
- edge_second: bfloat16 [128, 128], replicated, may hold values from -0.5 to 0.5
- edge_third: bfloat16 [128, 128], replicated, may hold values from -0.5 to 0.5
- contact_first: bfloat16 [384, 128], replicated, may hold values from -0.3125 to 0.3125
- contact_second: bfloat16 [128, 128], replicated, may hold values from -0.5 to 0.5
- contact_third: bfloat16 [128, 128], replicated, may hold values from -0.5 to 0.5
- node_first: bfloat16 [384, 128], replicated, may hold values from -0.3125 to 0.3125
- node_second: bfloat16 [128, 128], replicated, may hold values from -0.5 to 0.5
- node_third: bfloat16 [128, 128], replicated, may hold values from -0.5 to 0.5
Outputs:
- new_nodes: bfloat16 [262144, 128], P(('group', 'dom'))
- new_mesh_edges: bfloat16 [1572864, 128], P(('group', 'dom'))
- new_contact_edges: bfloat16 [16384, 64, 128], P(('group', 'dom'))
Inputs may be any that keep to these rules, and one draw needn't show every extreme that they name: `mesh_src`: the source of device d's edge k (target node n = k // 6) lies in table rows 128 * (n // 128) to 128 * (n // 128) + 128 + 2 * 256 - 1. `contact_counts`: every device sends exactly 64 to some device, and some device receives exactly 64 from every device.
All inputs are finite; a program needn't handle non-finite values.
Results may differ from a plain program's by a relative error of at most 0.0058.
Values may be sent and summed in bfloat16 or wider, within the bound.
No kernel may reach another device: no remote copies, remote signals or barrier semaphores. Data moves between devices by JAX's collectives and lax.ppermute only.
A program may use at most 128 MiB of HBM per device.

v0:
```python
import functools

import jax
import jax.numpy as jnp
from jax import lax
from jax.experimental import pallas as pl
from jax.experimental.pallas import tpu as pltpu
from jax.sharding import PartitionSpec as P

W = 128
BLOCK = 128
HALO = 256
SPLIT = 2
F32 = jnp.float32
BF16 = jnp.bfloat16
ANY = pl.BlockSpec(memory_space=pl.ANY)
VMEM = pl.BlockSpec(memory_space=pltpu.VMEM)
HBM = pl.BlockSpec(memory_space=pltpu.HBM)
SMEM = pl.BlockSpec(memory_space=pltpu.SMEM)


def dot(a, b):
    return jnp.dot(a, b, preferred_element_type=F32)


def params(mib=60):
    return pltpu.CompilerParams(vmem_limit_bytes=mib << 20)


def cost(flops, moved, transcendentals=0):
    return pl.CostEstimate(flops=flops, bytes_accessed=moved, transcendentals=transcendentals)


def shape(rows, dtype=BF16, width=W):
    return jax.ShapeDtypeStruct((rows, width), dtype)


def pipeline(stages, count):
    held = {}
    for step in range(count + len(stages) - 1):
        given = {}
        for s, stage in enumerate(stages):
            chunk = step - s
            if 0 <= chunk < count:
                given[s] = stage(chunk, held.get(s - 1))
        held = given


def cut(chunk, size):
    return slice(chunk * size, (chunk + 1) * size)


def pair(x):
    half = x.shape[0] // 2
    return jnp.concatenate([x[:half], x[half:]], axis=1)


def unpair(x):
    return jnp.concatenate([x[:, :W], x[:, W:]], axis=0)


def twice(w):
    zero = jnp.zeros_like(w)
    return jnp.concatenate(
        [jnp.concatenate([w, zero], axis=1), jnp.concatenate([zero, w], axis=1)], axis=0
    )


def fill(weights_ref, second, third):
    wide = third.astype(F32)
    wide = wide - jnp.mean(wide, axis=1, keepdims=True)
    high = wide.astype(BF16)
    weights_ref[0] = twice(second)
    weights_ref[1] = twice(high)
    weights_ref[2] = twice((wide - high.astype(F32)).astype(BF16))
    weights_ref[3] = twice(jnp.full((W, W), 1.0 / W, BF16))


def network(weights_ref):
    def second(chunk, summed):
        return dot(jnp.maximum(summed, 0.0).astype(BF16), weights_ref[0])

    def third(chunk, summed):
        two = jnp.maximum(summed, 0.0).astype(BF16)
        return dot(two, weights_ref[1]) + dot(two, weights_ref[2])

    def spread(chunk, centred):
        return centred, dot((centred * centred).astype(BF16), weights_ref[3])

    return [second, third, spread]


def normal(given):
    centred, variance = given
    return centred * lax.rsqrt(variance + 1e-05)


def columns(rows):
    count, length = rows.shape
    return jnp.concatenate(
        [jnp.broadcast_to(rows[i : i + 1], (W, length)).T for i in range(count)], axis=0
    )


def columns_down(rows):
    length, count = rows.shape
    return jnp.concatenate(
        [jnp.broadcast_to(rows[:, i : i + 1], (length, W)) for i in range(count)], axis=0
    )


def one_hot(column, span):
    lane = lax.broadcasted_iota(jnp.int32, (column.shape[0], W), 1).astype(jnp.int16)
    short = column.astype(jnp.int16)
    one, zero = jnp.ones((), BF16), jnp.zeros((), BF16)
    return jnp.concatenate(
        [
            jnp.where(short == lane + jnp.int16(first), one, zero)
            for first in range(0, span, W)
        ],
        axis=1,
    )


def picking(column, nodes_ref, use):
    span = nodes_ref.shape[0] // SPLIT
    table = jnp.concatenate([nodes_ref[cut(r, span)] for r in range(SPLIT)], axis=1)

    def select(chunk, unused):
        numbers = column(chunk)
        return one_hot(numbers & (span - 1), span), numbers >> (span.bit_length() - 1)

    def multiply(chunk, given):
        hot, part = given
        result = dot(hot, table)
        out = result[:, :W]
        for r in range(1, SPLIT):
            out = jnp.where(part == r, result[:, r * W : (r + 1) * W], out)
        return use(chunk, out.astype(BF16))

    return [select, multiply]


def gather_kernel(rows_ref, nodes_ref, out_ref, rows_buf, nodes_buf, out_buf, sem):
    fetch_rows = pltpu.make_async_copy(rows_ref, rows_buf, sem.at[0])
    fetch_nodes = pltpu.make_async_copy(nodes_ref, nodes_buf, sem.at[1])
    fetch_rows.start()
    fetch_nodes.start()
    fetch_rows.wait()
    fetch_nodes.wait()
    peers = 8
    length, count = rows_buf.shape
    size = peers * length

    def use(chunk, rows):
        out_buf[cut(chunk, size)] = rows
        pltpu.make_async_copy(
            out_buf.at[cut(chunk, size)], out_ref.at[cut(chunk, size)], sem.at[2]
        ).start()

    def column(chunk):
        return columns_down(rows_buf[:, cut(chunk, peers)])

    pipeline(picking(column, nodes_buf, use), count // peers)
    pltpu.make_async_copy(out_buf, out_ref, sem.at[2]).wait()


def gather_rows(rows, nodes):
    total = rows.size
    return pl.pallas_call(
        gather_kernel,
        in_specs=[HBM, HBM],
        out_specs=HBM,
        out_shape=shape(total),
        scratch_shapes=[
            pltpu.VMEM(rows.shape, rows.dtype),
            pltpu.VMEM(nodes.shape, BF16),
            pltpu.VMEM((total, W), BF16),
            pltpu.SemaphoreType.DMA((3,)),
        ],
        compiler_params=params(),
        cost_estimate=cost(2 * total * nodes.shape[0] * W, total * W * 2),
    )(rows, nodes)


def rim_kernel(rows_ref, nodes_ref, first_ref, last_ref):
    lists = HALO // W
    outs = (first_ref, last_ref)

    def use(chunk, rows):
        outs[chunk][...] = rows

    def column(chunk):
        return columns(rows_ref[cut(chunk, lists)])

    pipeline(picking(column, nodes_ref, use), len(outs))


def rim_rows(rows, nodes):
    return pl.pallas_call(
        rim_kernel,
        in_specs=[VMEM, VMEM],
        out_specs=[VMEM, VMEM],
        out_shape=[shape(HALO)] * 2,
        compiler_params=params(),
        cost_estimate=cost(2 * rows.size * nodes.shape[0] * W, (rows.size + nodes.shape[0]) * 256),
    )(rows, nodes)


def partner_kernel(
    rows_ref, nodes_ref, edges_ref, first_ref, out_ref, out_buf, sem,
):
    weights = jnp.concatenate([first_ref[:W], first_ref[2 * W :]], axis=0)
    peers = 8
    length, count = rows_ref.shape
    size = peers * length

    def column(chunk):
        return columns_down(rows_ref[:, cut(chunk, peers)])

    def add(chunk, latent):
        here = cut(chunk, size)
        out_buf[here] = dot(jnp.concatenate([edges_ref[here], latent], axis=1), weights)
        pltpu.make_async_copy(out_buf.at[here], out_ref.at[here], sem.at[0]).start()

    pipeline(picking(column, nodes_ref, lambda chunk, rows: rows) + [add], count // peers)
    pltpu.make_async_copy(out_buf, out_ref, sem.at[0]).wait()


def partner_part(rows, nodes, edges, first):
    total = rows.size
    return pl.pallas_call(
        partner_kernel,
        in_specs=[VMEM] * 4,
        out_specs=HBM,
        out_shape=shape(total, F32),
        scratch_shapes=[
            pltpu.VMEM((total, W), F32),
            pltpu.SemaphoreType.DMA((1,)),
        ],
        compiler_params=params(),
        cost_estimate=cost(2 * total * (nodes.shape[0] + 2 * W) * W, total * W * 8),
    )(rows, nodes, edges, first)


class Fetch:
    def __init__(self, source, target, sem, parts=1):
        self.rows = source.shape[0] // parts
        self.copies = [
            pltpu.make_async_copy(
                source.at[cut(i, self.rows)], target.at[cut(i, self.rows)], sem.at[i]
            )
            for i in range(parts)
        ]
        self.ready = 0

    def start(self, i=0):
        self.copies[i].start()

    def until(self, rows):
        while self.ready < len(self.copies) and self.ready * self.rows < rows:
            self.copies[self.ready].wait()
            self.ready += 1


def contact_kernel(
    capacity, counts_ref, arrived_ref, part_hbm, edges_hbm, first_ref, second_ref, third_ref, lower_ref, upper_ref,
    after_ref, message_ref, part_ref, edges_ref, weights_ref, in_sem,
):
    size = 512
    peers = size // capacity
    parts = 2
    slot = lax.broadcasted_iota(jnp.int32, (capacity, W), 0)
    part = Fetch(part_hbm, part_ref, in_sem.at[0], parts)
    edges = Fetch(edges_hbm, edges_ref, in_sem.at[1], parts)
    for i in range(parts):
        part.start(i)
        edges.start(i)
    fill(weights_ref, second_ref[...], third_ref[...])
    weights_ref[4] = twice(first_ref[W : 2 * W])

    def first(chunk, unused):
        for fetch in (part, edges):
            fetch.until((chunk + 1) * size)
        came = pair(arrived_ref[cut(chunk, size)])
        return dot(came, weights_ref[4]) + pair(part_ref[cut(chunk, size)])

    def finish(chunk, given):
        here = cut(chunk, size)
        new = edges_ref[here].astype(F32) + unpair(normal(given))
        sent = [
            jnp.where(slot < counts_ref[chunk * peers + p], new[cut(p, capacity)], 0.0)
            for p in range(peers)
        ]
        message_ref[here] = jnp.concatenate(sent, axis=0).astype(BF16)

    pipeline([first] + network(weights_ref) + [finish], arrived_ref.shape[0] // size)


def contact_rest(counts, arrived, part, edges, weights, lower, upper, after, capacity):
    total = arrived.shape[0]
    return pl.pallas_call(
        functools.partial(contact_kernel, capacity),
        in_specs=[SMEM, VMEM, HBM, HBM, VMEM, VMEM, VMEM, ANY, ANY, ANY],
        out_specs=VMEM,
        out_shape=shape(total),
        scratch_shapes=[
            pltpu.VMEM((total, W), F32),
            pltpu.VMEM((total, W), BF16),
            pltpu.VMEM((5, 2 * W, 2 * W), BF16),
            pltpu.SemaphoreType.DMA((3, 8)),
        ],
        compiler_params=params(48),
        cost_estimate=cost(2 * total * 4 * W * W, total * W * 14, total * W),
    )(counts, arrived, part, edges, *weights, lower, upper, after)


def adding(rows_ref, values_ref, total_ref, also=lambda chunk, values: None):
    span = total_ref.shape[0]
    shift = span.bit_length() - 1
    lists = 8
    height = 256
    zero, one = jnp.zeros((), BF16), jnp.ones((), BF16)
    index = lax.broadcasted_iota(jnp.int32, (height, W), 0).astype(jnp.int16)

    def select(chunk, unused):
        rows = rows_ref[cut(chunk, lists)]
        values = values_ref[cut(chunk, lists * W)]
        also(chunk, values)
        part = columns(rows >> shift).astype(jnp.int16)
        wide = jnp.concatenate(
            [jnp.where(part == jnp.int16(r), values, zero) for r in range(SPLIT)], axis=1
        )
        low = rows & (span - 1)
        across = [
            jnp.concatenate(
                [jnp.broadcast_to(low[i : i + 1], (16, W)).astype(jnp.int16)] * (height // 16),
                axis=0,
            )
            for i in range(lists)
        ]
        hot = [
            jnp.concatenate(
                [jnp.where(row == index + jnp.int16(first), one, zero) for row in across], axis=1
            )
            for first in range(0, span, height)
        ]
        return hot, wide

    def multiply(chunk, given):
        hot, wide = given
        for k, rows in enumerate(hot):
            total_ref[cut(k, height)] += dot(rows, wide)

    return [select, multiply], rows_ref.shape[0] // lists


def received_kernel(
    capacity, counts_ref, edges_ref, rows_ref, values_ref, nodes_ref, inner_ref, outer_ref, first_ref, second_ref, third_ref,
    sums_hbm, prepared_hbm, new_hbm, total_ref, part_ref, weights_ref, new_buf, sem,
):
    total_ref[...] = jnp.zeros_like(total_ref)
    fill(weights_ref, second_ref[...], third_ref[...])
    weights_ref[4] = twice(first_ref[2 * W :])
    edge = outer_ref.shape[0] // 2
    mesh = jnp.concatenate([outer_ref[:edge], inner_ref[...], outer_ref[edge:]], axis=0)
    part_ref[...] = dot(pair(nodes_ref[...]), twice(first_ref[:W])) + dot(
        pair(mesh), twice(first_ref[W : 2 * W])
    )
    span = total_ref.shape[0]
    keep = [
        pltpu.make_async_copy(part_ref, sums_hbm.at[span : 2 * span], sem.at[0]),
        pltpu.make_async_copy(weights_ref, prepared_hbm.at[: weights_ref.shape[0]], sem.at[1]),
    ]
    for copy in keep:
        copy.start()
    slot = lax.broadcasted_iota(jnp.int32, (capacity, W), 0)

    def renew(chunk, values):
        size = values.shape[0]
        here = cut(chunk, size)
        edges = edges_ref[here].astype(F32)
        sent = values.astype(F32)
        peers = size // capacity
        new = [
            jnp.where(
                slot < counts_ref[chunk * peers + p], sent[cut(p, capacity)], edges[cut(p, capacity)]
            )
            for p in range(peers)
        ]
        new_buf[here] = jnp.concatenate(new, axis=0).astype(BF16)
        pltpu.make_async_copy(new_buf.at[here], new_hbm.at[here], sem.at[3]).start()

    pipeline(*adding(rows_ref, values_ref, total_ref, renew))
    keep.append(pltpu.make_async_copy(new_buf, new_hbm, sem.at[3]))
    keep.append(pltpu.make_async_copy(total_ref, sums_hbm.at[:span], sem.at[2]))
    keep[-1].start()
    for copy in keep:
        copy.wait()


def received_sum(
    counts, edges, rows, values, nodes, inner, outer, first, second, third, capacity
):
    span = nodes.shape[0] // SPLIT
    return pl.pallas_call(
        functools.partial(received_kernel, capacity),
        in_specs=[SMEM] + [VMEM] * 9,
        out_specs=[HBM] * 3,
        out_shape=[
            shape(12 * span, F32, SPLIT * W),
            jax.ShapeDtypeStruct((96, 2 * W, 2 * W), BF16),
            shape(values.shape[0]),
        ],
        scratch_shapes=[
            pltpu.VMEM((span, SPLIT * W), F32),
            pltpu.VMEM((span, SPLIT * W), F32),
            pltpu.VMEM((5, 2 * W, 2 * W), BF16),
            pltpu.VMEM(values.shape, BF16),
            pltpu.SemaphoreType.DMA((4,)),
        ],
        compiler_params=params(),
        cost_estimate=cost(2 * values.shape[0] * nodes.shape[0] * W, values.size * 2),
    )(counts, edges, rows, values, nodes, inner, outer, first, second, third)


def node_kernel(
    rows_ref, values_ref, sums_hbm, prepared_hbm, nodes_ref, out_ref, total_ref, sums_ref,
    weights_ref, out_buf, in_sem, sem,
):
    span = total_ref.shape[0]
    sums = Fetch(sums_hbm.at[: 2 * span], sums_ref, in_sem.at[0])
    weights = Fetch(prepared_hbm.at[: weights_ref.shape[0]], weights_ref, in_sem.at[1])
    sums.start()
    weights.start()
    total_ref[...] = jnp.zeros_like(total_ref)
    pipeline(*adding(rows_ref, values_ref, total_ref))
    sums.until(1)
    weights.until(1)
    size = 256

    def first(chunk, unused):
        here = cut(chunk, size)
        world = (total_ref[here] + sums_ref[here]).astype(BF16)
        part = sums_ref[slice(span + chunk * size, span + (chunk + 1) * size)]
        return part + dot(world, weights_ref[4])

    def finish(chunk, given):
        update = normal(given)
        for r in range(SPLIT):
            here = slice(r * span + chunk * size, r * span + (chunk + 1) * size)
            new = nodes_ref[here].astype(F32) + update[:, r * W : (r + 1) * W]
            out_buf[here] = new.astype(BF16)
            pltpu.make_async_copy(out_buf.at[here], out_ref.at[here], sem.at[0]).start()

    pipeline([first] + network(weights_ref) + [finish], span // size)
    pltpu.make_async_copy(out_buf, out_ref, sem.at[0]).wait()


def node_update(rows, values, sums, prepared, nodes):
    span = nodes.shape[0] // SPLIT
    return pl.pallas_call(
        node_kernel,
        in_specs=[VMEM, VMEM, HBM, HBM, VMEM],
        out_specs=HBM,
        out_shape=shape(nodes.shape[0]),
        scratch_shapes=[
            pltpu.VMEM((span, SPLIT * W), F32),
            pltpu.VMEM((2 * span, SPLIT * W), F32),
            pltpu.VMEM((5, 2 * W, 2 * W), BF16),
            pltpu.VMEM(nodes.shape, BF16),
            pltpu.SemaphoreType.DMA((2, 1)),
            pltpu.SemaphoreType.DMA((1,)),
        ],
        compiler_params=params(48),
        cost_estimate=cost(2 * values.shape[0] * nodes.shape[0] * W, values.size * 4, nodes.size),
    )(rows, values, sums, prepared, nodes)


def mesh_stages(
    degree, blocks, table_ref, offset, source_ref, edges_ref, first_ref, weights_ref, target_ref,
    new_buf, new_ref, total_ref, sem,
):
    span = BLOCK + 2 * HALO
    here = degree * BLOCK
    edge_row = lax.broadcasted_iota(jnp.int32, (here, W), 0)
    base = lax.broadcasted_iota(jnp.int32, (here, W), 1) * degree
    near = (edge_row >= base) & (edge_row < base + degree)
    target_ref[...] = jnp.where(near, 1.0, 0.0).astype(BF16)
    down = lax.broadcasted_iota(jnp.int32, (BLOCK, here), 0) * degree
    across = lax.broadcasted_iota(jnp.int32, (BLOCK, here), 1)
    hold = jnp.where((across >= down) & (across < down + degree), 1.0, 0.0).astype(BF16)

    def select(chunk, unused):
        row = blocks[chunk] * BLOCK
        return one_hot(columns(source_ref[blocks[chunk]] - row), span)

    def latents(chunk, hot):
        row = blocks[chunk] * BLOCK - offset
        window = table_ref[row : row + span]
        own = table_ref[row + HALO : row + HALO + BLOCK]
        table = jnp.concatenate(
            [
                jnp.concatenate([window, jnp.zeros_like(window)], axis=1),
                jnp.concatenate([jnp.zeros_like(own), own], axis=1),
            ],
            axis=0,
        )
        return dot(jnp.concatenate([hot, target_ref[...]], axis=1), table).astype(BF16)

    def first(chunk, latent):
        edges = edges_ref[cut(blocks[chunk], here)]
        return pair(dot(jnp.concatenate([edges, latent], axis=1), first_ref[...]))

    def finish(chunk, given):
        edges = edges_ref[cut(blocks[chunk], here)]
        new = (edges.astype(F32) + unpair(normal(given))).astype(BF16)
        new_buf[cut(chunk, here)] = new
        pltpu.make_async_copy(
            new_buf.at[cut(chunk, here)], new_ref.at[cut(blocks[chunk], here)], sem
        ).start()
        return new

    def gather(chunk, new):
        total_ref[cut(chunk, BLOCK)] = dot(hold, new).astype(BF16)

    pipeline([select, latents, first] + network(weights_ref) + [finish, gather], len(blocks))
    pltpu.make_async_copy(new_buf, new_ref.at[: len(blocks) * here], sem).wait()


def inner_kernel(
    degree, blocks, source_ref, edges_ref, nodes_ref, first_ref, second_ref, third_ref, after_ref,
    new_ref, total_ref, token_ref, weights_ref, target_ref, new_buf, sem,
):
    token_ref[...] = jnp.zeros_like(token_ref)
    fill(weights_ref, second_ref[...], third_ref[...])
    mesh_stages(
        degree, blocks, nodes_ref, HALO, source_ref, edges_ref, first_ref, weights_ref, target_ref,
        new_buf, new_ref, total_ref, sem.at[0],
    )


def outer_kernel(
    degree, blocks, source_ref, edges_ref, nodes_ref, first_ref, second_ref, third_ref, after_ref,
    lower_ref, upper_ref, mesh_ref, new_ref, total_ref, weights_ref, target_ref, new_buf, sem,
    table_ref,
):
    count = nodes_ref.shape[0]
    fill(weights_ref, second_ref[...], third_ref[...])
    table_ref[:HALO] = lower_ref[...]
    table_ref[HALO : HALO + count] = nodes_ref[...]
    table_ref[HALO + count :] = upper_ref[...]
    mesh_stages(
        degree, blocks, table_ref, 0, source_ref, edges_ref, first_ref, weights_ref, target_ref,
        new_buf, new_ref, total_ref, sem.at[0],
    )


def mesh_update(kernel, blocks, source, edges, nodes, weights, after, extra=()):
    degree = edges.shape[0] // nodes.shape[0]
    here = degree * BLOCK
    rows = len(blocks) * here
    scratch = [
        pltpu.VMEM((4, 2 * W, 2 * W), BF16),
        pltpu.VMEM((here, W), BF16),
        pltpu.VMEM((rows, W), BF16),
        pltpu.SemaphoreType.DMA((1,)),
    ]
    if extra:
        scratch.append(pltpu.VMEM((nodes.shape[0] + 2 * HALO, W), BF16))
    return pl.pallas_call(
        functools.partial(kernel, degree, blocks),
        in_specs=[VMEM] * 6 + [ANY] + ([VMEM, VMEM, ANY] if extra else []),
        out_specs=[ANY, VMEM] + ([] if extra else [VMEM]),
        out_shape=[shape(edges.shape[0]), shape(len(blocks) * BLOCK)]
        + ([] if extra else [shape(16)]),
        scratch_shapes=scratch,
        input_output_aliases={9: 0} if extra else {},
        compiler_params=params(),
        cost_estimate=cost(2 * rows * 1800 * W, rows * W * 4, rows * W),
    )(source, edges, nodes, *weights, after, *extra)


def shards(
    nodes,
    mesh_edges,
    contact_edges,
    mesh_src,
    halo_rows,
    send_rows,
    partner_rows,
    contact_counts,
    edge_first,
    edge_second,
    edge_third,
    contact_first,
    contact_second,
    contact_third,
    node_first,
    node_second,
    node_third,
):
    axes = ("group", "dom")
    node_count = nodes.shape[0]
    degree = mesh_edges.shape[0] // node_count
    peers, capacity = send_rows.shape
    slots = peers * capacity

    outgoing = gather_rows(send_rows.T, nodes).reshape(peers, capacity, W)
    arrived = lax.all_to_all(outgoing, axes, split_axis=0, concat_axis=0, tiled=True)

    size = lax.axis_size("dom")
    to_lower, to_upper = rim_rows(halo_rows.reshape(-1, W), nodes)
    lower = lax.ppermute(to_upper, "dom", [(i, i + 1) for i in range(size - 1)])
    upper = lax.ppermute(to_lower, "dom", [(i + 1, i) for i in range(size - 1)])

    edges = contact_edges.reshape(slots, W)
    part = partner_part(
        partner_rows.T, nodes, edges, contact_first
    )
    blocks = node_count // BLOCK
    late = 2 * HALO // BLOCK
    inside = tuple(range(late, blocks - late))
    outside = tuple(range(late)) + tuple(range(blocks - late, blocks))
    source = mesh_src.reshape(blocks, degree, BLOCK)
    edge_weights = (edge_first, edge_second, edge_third)
    new_mesh, inner_total, token = mesh_update(
        inner_kernel, inside, source, mesh_edges, nodes, edge_weights, to_lower
    )

    device = lax.axis_index("group") * size + lax.axis_index("dom")
    counts = lax.dynamic_index_in_dim(contact_counts, device, 1, keepdims=False)
    message = contact_rest(
        counts, arrived.reshape(slots, W), part, edges,
        (contact_first, contact_second, contact_third), lower, upper,
        token, capacity
    )
    returned = lax.all_to_all(
        message.reshape(peers, capacity, W), axes, split_axis=0, concat_axis=0, tiled=True
    ).reshape(slots, W)

    new_mesh, outer_total = mesh_update(
        outer_kernel, outside, source, mesh_edges, nodes, edge_weights, message,
        (lower, upper, new_mesh),
    )
    sums, prepared, new_contacts = received_sum(
        counts, edges, partner_rows.reshape(-1, W), message, nodes, inner_total, outer_total,
        node_first, node_second, node_third, capacity,
    )
    new_nodes = node_update(
        send_rows.reshape(-1, W), returned, sums, prepared, nodes
    )
    return (new_nodes, new_mesh, new_contacts.reshape(peers, capacity, W))


def solution(mesh):
    split = P(("group", "dom"))
    in_specs = (split,) * 7 + (P(),) * 10
    return jax.shard_map(
        shards, mesh=mesh, in_specs=in_specs, out_specs=(split,) * 3, check_vma=False
    )
```

profile of v0, /device:TPU:1, one launch (start us, length us, event | category | flops | bytes accessed | tf_op | source)
XLA Modules:
  0.0 104.3 jit_solution(16342815602540269871)
XLA Ops:
  0.6 0.0 copy-start
  0.6 6.4 %shard_map.184 = bf16[8192,128]{1,0:T(8,128)(2,1)} custom-call(s32[64,128]{1,0:T(8,128)} %bitcast.16, bf16[2048,128]{1,0:T(8,128)(2,1)} %nodes_ref.13), custom_call_target="tpu_custom_call" | custom-call | flops 4294967296 | bytes 2097152 | tf_op jit(solution)/shard_map/pallas_call | solution.py:170
  7.1 0.0 copy-start.13
  7.1 0.0 copy-start.10
  7.1 11.5 %all-to-all-start = ((bf16[128,64,128]{2,1,0:T(8,128)(2,1)}), bf16[128,64,128]{2,1,0:T(8,128)(2,1)S(1)}, u32[]{:S(2)}, u32[]{:S(2)}) async-start(bf16[128,64,128]{2,1,0:T(8,128)(2,1)} %bitcast.14), calls=%async_computation | async-start | bytes 4194304 | tf_op jit(solution)/shard_map/all_to_all | solution.py:610
  18.6 0.0 copy-done.13
  18.6 0.6 reshape.40.rows_ref
  19.2 2.2 %shard_map.186 = (bf16[256,128]{1,0:T(8,128)(2,1)}, bf16[256,128]{1,0:T(8,128)(2,1)}) custom-call(s32[4,128]{1,0:T(4,128)} %reshape.40.rows_ref, bf16[2048,128]{1,0:T(8,128)(2,1)} %nodes_ref.13), custom_call_target="tpu_custom_call" | custom-call | flops 268435456 | bytes 655360 | tf_op jit(solution)/shard_map/pallas_call | solution.py:200
  21.4 3.0 %collective-permute-start.1 = (bf16[256,128]{1,0:T(8,128)(2,1)}, bf16[256,128]{1,0:T(8,128)(2,1)S(1)}, u32[]{:S(2)}, u32[]{:S(2)}) collective-permute-start(bf16[256,128]{1,0:T(8,128)(2,1)} %get-tuple-element.14.after_ref), channel_id=1, source_target_pairs={{1,0},{2,1},{3,2},{4,3},{5,4},{6,5},{7,6},{8,7},{9,8},{10,9},{11,1... | collective-permute-start | bytes 196616 | tf_op jit(solution)/shard_map/ppermute | solution.py:615
  24.4 2.8 %collective-permute-start = (bf16[256,128]{1,0:T(8,128)(2,1)}, bf16[256,128]{1,0:T(8,128)(2,1)S(1)}, u32[]{:S(2)}, u32[]{:S(2)}) collective-permute-start(bf16[256,128]{1,0:T(8,128)(2,1)} %get-tuple-element.13), channel_id=1, source_target_pairs={{0,1},{1,2},{2,3},{3,4},{4,5},{5,6},{6,7},{7,8},{8,9},{9,10},{10,1... | collective-permute-start | bytes 196616 | tf_op jit(solution)/shard_map/ppermute | solution.py:614
  27.1 0.0 copy-done.10
  27.2 0.6 reshape.41.source_ref
  27.8 8.2 %shard_map.185.part_hbm = f32[8192,128]{1,0:T(8,128)} custom-call(s32[64,128]{1,0:T(8,128)} %bitcast.15, bf16[2048,128]{1,0:T(8,128)(2,1)} %nodes_ref.13, bf16[8192,128]{1,0:T(8,128)(2,1)} %bitcast.11, bf16[384,128]{1,0:T(8,128)(2,1)} %first_ref.7), custom_call_target="tpu_custom_call" | custom-call | flops 4831838208 | bytes 8388608 | tf_op jit(solution)/shard_map/pallas_call | solution.py:232
  36.0 0.0 copy-start.3
  36.0 0.0 copy-start.6
  36.1 0.0 copy-start.7
  36.1 9.4 %shard_map.187 = (bf16[12288,128]{1,0:T(8,128)(2,1)}, bf16[1024,128]{1,0:T(8,128)(2,1)}, bf16[16,128]{1,0:T(8,128)(2,1)}) custom-call(s32[16,6,128]{2,1,0:T(8,128)} %reshape.41.source_ref, bf16[12288,128]{1,0:T(8,128)(2,1)} %edges_ref.3, bf16[2048,128]{1,0:T(8,128)(2,1)} %nodes_ref.13, bf16[384,128]{1,0:T(8,128)(2,1)} %first_ref.8, ...), custom_call_target="tpu_custom_call" | custom-call | flops 2831155200 | bytes 3145728 | tf_op jit(solution)/shard_map/pallas_call | solution.py:571
  45.5 0.0 copy-done
  45.5 0.2 dynamic-slice_reduce_fusion.counts_ref
  45.7 0.0 copy-start.9
  45.7 0.0 collective-permute-done.1.upper_ref
  45.7 0.0 copy-start.4
  45.7 0.0 collective-permute-done.lower_ref
  45.7 0.0 copy-start.5
  45.7 3.2 %all-to-all-done = bf16[128,64,128]{2,1,0:T(8,128)(2,1)S(1)} async-done(((bf16[128,64,128]{2,1,0:T(8,128)(2,1)}), bf16[128,64,128]{2,1,0:T(8,128)(2,1)S(1)}, u32[]{:S(2)}, u32[]{:S(2)}) %all-to-all-start) | async-done | bytes 2097184 | tf_op jit(solution)/shard_map/all_to_all | solution.py:610
  48.9 0.0 copy-done.3
  49.0 0.0 copy-done.6
  49.0 0.0 copy-done.7
  49.0 0.0 copy-start.8
  49.0 0.7 copy-done.8
  49.6 6.2 %shard_map.188.after_ref.values_ref = bf16[8192,128]{1,0:T(8,128)(2,1)S(1)} custom-call(s32[128]{0:T(128)S(1)} %dynamic-slice_reduce_fusion.counts_ref, bf16[8192,128]{1,0:T(8,128)(2,1)S(1)} %bitcast.8, f32[8192,128]{1,0:T(8,128)} %shard_map.185.part_hbm, bf16[8192,128]{1,0:T(8,128)(2,1)} %bitcast.12, bf16[384,128]{1,0:T(8,128)(2,1)S(1)} %copy-done.3, ...), custom_call_target="tpu_custom_call" | custom-call | flops 1073741824 | bytes 14680064 | tf_op jit(solution)/shard_map/pallas_call | solution.py:302
  55.9 0.0 copy-done.9
  55.9 0.0 copy-done.4
  55.9 0.0 copy-done.5
  55.9 0.0 copy-start.1
  55.9 1.4 %copy-done.1 = bf16[8192,128]{1,0:T(8,128)(2,1)} copy-done((bf16[8192,128]{1,0:T(8,128)(2,1)}, bf16[8192,128]{1,0:T(8,128)(2,1)S(1)}, u32[]{:S(2)}) %copy-start.1) | copy-done | bytes 2097176
  57.3 8.2 %all-to-all-start.1 = ((bf16[128,64,128]{2,1,0:T(8,128)(2,1)}), bf16[128,64,128]{2,1,0:T(8,128)(2,1)S(1)}, u32[]{:S(2)}, u32[]{:S(2)}) async-start(bf16[128,64,128]{2,1,0:T(8,128)(2,1)} %bitcast.9), calls=%async_computation.1 | async-start | bytes 4194304 | tf_op jit(solution)/shard_map/all_to_all | solution.py:638
  65.5 0.0 copy-done.11
  65.5 0.1 copy.24
  65.6 0.1 copy.23
  65.7 0.7 reshape.44.rows_ref
  66.4 0.1 reshape.36.rows_ref
  66.4 9.4 %shard_map.189 = (bf16[12288,128]{1,0:T(8,128)(2,1)}, bf16[1024,128]{1,0:T(8,128)(2,1)}) custom-call(s32[16,6,128]{2,1,0:T(8,128)} %reshape.41.source_ref, bf16[12288,128]{1,0:T(8,128)(2,1)} %edges_ref.3, bf16[2048,128]{1,0:T(8,128)(2,1)} %nodes_ref.13, bf16[384,128]{1,0:T(8,128)(2,1)} %first_ref.8, ...), custom_call_target="tpu_custom_call", output_to_operand_aliasing={{0}: (9, {})} | custom-call | flops 2831155200 | bytes 3145728 | tf_op jit(solution)/shard_map/pallas_call | solution.py:571
  75.9 0.0 copy-start.2
  75.9 9.5 %shard_map.190 = (f32[12288,256]{1,0:T(8,128)}, bf16[96,256,256]{2,1,0:T(8,128)(2,1)}, bf16[8192,128]{1,0:T(8,128)(2,1)}) custom-call(s32[128]{0:T(128)} %copy-done.9, bf16[8192,128]{1,0:T(8,128)(2,1)} %bitcast.13, s32[64,128]{1,0:T(8,128)} %reshape.44.rows_ref, bf16[8192,128]{1,0:T(8,128)(2,1)} %copy-done.1, bf16[2048,128]{1,0:T(8,128)(2,1)} %nodes_ref.13, ...), custom_call_target="tpu_custom_call" | custom-call | flops 4294967296 | bytes 2097152 | tf_op jit(solution)/shard_map/pallas_call | solution.py:406
  85.4 10.6 %all-to-all-done.1 = bf16[128,64,128]{2,1,0:T(8,128)(2,1)S(1)} async-done(((bf16[128,64,128]{2,1,0:T(8,128)(2,1)}), bf16[128,64,128]{2,1,0:T(8,128)(2,1)S(1)}, u32[]{:S(2)}, u32[]{:S(2)}) %all-to-all-start.1) | async-done | bytes 2097184 | tf_op jit(solution)/shard_map/all_to_all | solution.py:638
  96.0 0.0 copy-done.2
  96.0 8.1 %shard_map.191 = bf16[2048,128]{1,0:T(8,128)(2,1)} custom-call(s32[64,128]{1,0:T(8,128)S(1)} %reshape.36.rows_ref, bf16[8192,128]{1,0:T(8,128)(2,1)S(1)} %bitcast.10, f32[12288,256]{1,0:T(8,128)} %get-tuple-element.19.sums_hbm, bf16[96,256,256]{2,1,0:T(8,128)(2,1)} %get-tuple-element.20.prepared_hbm, bf16[2048,128]{1,0:T(8,128)(2,1)S(1)} %copy-done.2), custom_call_target="tpu_custom_call" | custom-call | flops 4294967296 | bytes 4194304 | tf_op jit(solution)/shard_map/pallas_call | solution.py:462
  (3 shorter events, 0.0 us)
Async XLA Ops:
  0.6 44.9 %copy-start = (s32[128,128]{1,0:T(8,128)S(1)}, s32[128,128]{1,0:T(8,128)}, u32[]{:S(2)}) copy-start(s32[128,128]{1,0:T(8,128)} %param.24) | copy-start | bytes 196612
  7.1 11.5 %copy-start.13 = (s32[2,256]{1,0:T(2,128)S(1)}, s32[2,256]{1,0:T(2,128)}, u32[]{:S(2)}) copy-start(s32[2,256]{1,0:T(2,128)} %param.21) | copy-start | bytes 6148
  7.1 20.1 %copy-start.10 = (s32[12288]{0:T(1024)S(1)}, s32[12288]{0:T(1024)}, u32[]{:S(2)}) copy-start(s32[12288]{0:T(1024)} %param.20) | copy-start | bytes 147460
  7.1 41.9 %all-to-all-start = ((bf16[128,64,128]{2,1,0:T(8,128)(2,1)}), bf16[128,64,128]{2,1,0:T(8,128)(2,1)S(1)}, u32[]{:S(2)}, u32[]{:S(2)}) async-start(bf16[128,64,128]{2,1,0:T(8,128)(2,1)} %bitcast.14), calls=%async_computation | async-start | bytes 4194304 | tf_op jit(solution)/shard_map/all_to_all | solution.py:610
  21.4 24.3 %collective-permute-start.1 = (bf16[256,128]{1,0:T(8,128)(2,1)}, bf16[256,128]{1,0:T(8,128)(2,1)S(1)}, u32[]{:S(2)}, u32[]{:S(2)}) collective-permute-start(bf16[256,128]{1,0:T(8,128)(2,1)} %get-tuple-element.14.after_ref), channel_id=1, source_target_pairs={{1,0},{2,1},{3,2},{4,3},{5,4},{6,5},{7,6},{8,7},{9,8},{10,9},{11,1... | collective-permute-start | bytes 196616 | tf_op jit(solution)/shard_map/ppermute | solution.py:615
  24.4 21.3 %collective-permute-start = (bf16[256,128]{1,0:T(8,128)(2,1)}, bf16[256,128]{1,0:T(8,128)(2,1)S(1)}, u32[]{:S(2)}, u32[]{:S(2)}) collective-permute-start(bf16[256,128]{1,0:T(8,128)(2,1)} %get-tuple-element.13), channel_id=1, source_target_pairs={{0,1},{1,2},{2,3},{3,4},{4,5},{5,6},{6,7},{7,8},{8,9},{9,10},{10,1... | collective-permute-start | bytes 196616 | tf_op jit(solution)/shard_map/ppermute | solution.py:614
  36.0 12.9 %copy-start.3 = (bf16[384,128]{1,0:T(8,128)(2,1)S(1)}, bf16[384,128]{1,0:T(8,128)(2,1)}, u32[]{:S(2)}) copy-start(bf16[384,128]{1,0:T(8,128)(2,1)} %first_ref.7) | copy-start | bytes 294916
  36.0 12.9 %copy-start.6 = (bf16[128,128]{1,0:T(8,128)(2,1)S(1)}, bf16[128,128]{1,0:T(8,128)(2,1)}, u32[]{:S(2)}) copy-start(bf16[128,128]{1,0:T(8,128)(2,1)} %second_ref.5) | copy-start | bytes 98308
  36.1 12.9 %copy-start.7 = (bf16[128,128]{1,0:T(8,128)(2,1)S(1)}, bf16[128,128]{1,0:T(8,128)(2,1)}, u32[]{:S(2)}) copy-start(bf16[128,128]{1,0:T(8,128)(2,1)} %third_ref.5) | copy-start | bytes 98308
  45.7 10.2 %copy-start.9 = (s32[128]{0:T(128)}, s32[128]{0:T(128)S(1)}, u32[]{:S(2)}) copy-start(s32[128]{0:T(128)S(1)} %dynamic-slice_reduce_fusion.counts_ref) | copy-start | bytes 1540
  45.7 10.2 %copy-start.4 = (bf16[256,128]{1,0:T(8,128)(2,1)}, bf16[256,128]{1,0:T(8,128)(2,1)S(1)}, u32[]{:S(2)}) copy-start(bf16[256,128]{1,0:T(8,128)(2,1)S(1)} %collective-permute-done.1.upper_ref) | copy-start | bytes 196612
  45.7 10.2 %copy-start.5 = (bf16[256,128]{1,0:T(8,128)(2,1)}, bf16[256,128]{1,0:T(8,128)(2,1)S(1)}, u32[]{:S(2)}) copy-start(bf16[256,128]{1,0:T(8,128)(2,1)S(1)} %collective-permute-done.lower_ref) | copy-start | bytes 196612
  49.0 0.7 copy-start.8
  55.9 1.4 %copy-start.1 = (bf16[8192,128]{1,0:T(8,128)(2,1)}, bf16[8192,128]{1,0:T(8,128)(2,1)S(1)}, u32[]{:S(2)}) copy-start(bf16[8192,128]{1,0:T(8,128)(2,1)S(1)} %shard_map.188.after_ref.values_ref) | copy-start | bytes 6291460
  57.3 8.2 %copy-start.11 = (s32[128,64]{0,1:T(8,128)S(1)}, s32[128,64]{0,1:T(8,128)}, u32[]{:S(2)}) copy-start(s32[128,64]{0,1:T(8,128)} %param.23) | copy-start | bytes 98308
  57.3 8.3 %copy-start.12 = (s32[128,64]{0,1:T(8,128)S(1)}, s32[128,64]{0,1:T(8,128)}, u32[]{:S(2)}) copy-start(s32[128,64]{0,1:T(8,128)} %param.22) | copy-start | bytes 98308
  57.3 38.7 %all-to-all-start.1 = ((bf16[128,64,128]{2,1,0:T(8,128)(2,1)}), bf16[128,64,128]{2,1,0:T(8,128)(2,1)S(1)}, u32[]{:S(2)}, u32[]{:S(2)}) async-start(bf16[128,64,128]{2,1,0:T(8,128)(2,1)} %bitcast.9), calls=%async_computation.1 | async-start | bytes 4194304 | tf_op jit(solution)/shard_map/all_to_all | solution.py:638
  75.9 20.1 %copy-start.2 = (bf16[2048,128]{1,0:T(8,128)(2,1)S(1)}, bf16[2048,128]{1,0:T(8,128)(2,1)}, u32[]{:S(2)}) copy-start(bf16[2048,128]{1,0:T(8,128)(2,1)} %nodes_ref.13) | copy-start | bytes 1572868
where the time goes:
time: 105 us; the launch traced here: 104 us
  Pallas kernels  59.5 us (57%)
  starting transfers between devices  25.4 us (24%)
  waiting for transfers between devices  13.8 us (13%)
  local copies, waits for them, and re-layouts  4.45 us (4%)
  between operations  1.11 us (1%)
    pallas_call x2, Pallas kernels, mesh_update(): pl.pallas_call(functools.partial(kernel, degree, blocks), in_specs=[VMEM]...  18.8 us
    all_to_all x1, starting transfers between devices, shards(): lax.all_to_all(outgoing, axes, split_axis=0, concat_axis=0, tiled=True)  11.5 us
    all_to_all x1, waiting for transfers between devices, shards(): lax.all_to_all(message.reshape(peers, capacity, W), axes, split_axis=0, c...  10.6 us
    pallas_call x1, Pallas kernels, received_sum(): pl.pallas_call(functools.partial(received_kernel, capacity), in_specs=[SM...  9.5 us
    pallas_call x1, Pallas kernels, partner_part(): pl.pallas_call(partner_kernel, in_specs=[VMEM] * 4, out_specs=HBM, out_sh...  8.24 us
    all_to_all x1, starting transfers between devices, shards(): lax.all_to_all(message.reshape(peers, capacity, W), axes, split_axis=0, c...  8.15 us
    pallas_call x1, Pallas kernels, node_update(): pl.pallas_call(node_kernel, in_specs=[VMEM, VMEM, HBM, HBM, VMEM], out_sp...  8.07 us
    pallas_call x1, Pallas kernels, gather_rows(): pl.pallas_call(gather_kernel, in_specs=[HBM, HBM], out_specs=HBM, out_sha...  6.41 us
  transfers between devices with their start and end apart: 4, of which 2 were waited for; matrix products, arithmetic and copies ran while one was open for 2% of the time, Pallas kernels for 37%

commit v1 on v0

--- a/solution.py
+++ b/solution.py
@@ -275,18 +275,19 @@
     edges = Fetch(edges_hbm, edges_ref, in_sem.at[1], parts)
     for i in range(parts):
         part.start(i)
+    for i in range(parts):
         edges.start(i)
     fill(weights_ref, second_ref[...], third_ref[...])
     weights_ref[4] = twice(first_ref[W : 2 * W])
 
     def first(chunk, unused):
-        for fetch in (part, edges):
-            fetch.until((chunk + 1) * size)
+        part.until((chunk + 1) * size)
         came = pair(arrived_ref[cut(chunk, size)])
         return dot(came, weights_ref[4]) + pair(part_ref[cut(chunk, size)])
 
     def finish(chunk, given):
         here = cut(chunk, size)
+        edges.until((chunk + 1) * size)
         new = edges_ref[here].astype(F32) + unpair(normal(given))
         sent = [
             jnp.where(slot < counts_ref[chunk * peers + p], new[cut(p, capacity)], 0.0)
@@ -318,7 +319,7 @@
 def adding(rows_ref, values_ref, total_ref, also=lambda chunk, values: None):
     span = total_ref.shape[0]
     shift = span.bit_length() - 1
-    lists = 8
+    lists = 4
     height = 256
     zero, one = jnp.zeros((), BF16), jnp.ones((), BF16)
     index = lax.broadcasted_iota(jnp.int32, (height, W), 0).astype(jnp.int16)

time: 105 us -> 105 us (level)
  no operation moved by 1% of the time
where the time goes in v1:
time: 105 us
  Pallas kernels  59.7 us (57%)
  starting transfers between devices  25.4 us (24%)
  waiting for transfers between devices  13.9 us (13%)
  local copies, waits for them, and re-layouts  4.45 us (4%)
  between operations  1.11 us (1%)
    pallas_call x2, Pallas kernels, mesh_update(): pl.pallas_call(functools.partial(kernel, degree, blocks), in_specs=[VMEM]...  18.8 us
    all_to_all x1, starting transfers between devices, shards(): lax.all_to_all(outgoing, axes, split_axis=0, concat_axis=0, tiled=True)  11.5 us
    all_to_all x1, waiting for transfers between devices, shards(): lax.all_to_all(message.reshape(peers, capacity, W), axes, split_axis=0, c...  10.7 us
    pallas_call x1, Pallas kernels, received_sum(): pl.pallas_call(functools.partial(received_kernel, capacity), in_specs=[SM...  9.44 us
    pallas_call x1, Pallas kernels, partner_part(): pl.pallas_call(partner_kernel, in_specs=[VMEM] * 4, out_specs=HBM, out_sh...  8.24 us
    all_to_all x1, starting transfers between devices, shards(): lax.all_to_all(message.reshape(peers, capacity, W), axes, split_axis=0, c...  8.15 us
    pallas_call x1, Pallas kernels, node_update(): pl.pallas_call(node_kernel, in_specs=[VMEM, VMEM, HBM, HBM, VMEM], out_sp...  7.97 us
    pallas_call x1, Pallas kernels, contact_rest(): pl.pallas_call(functools.partial(contact_kernel, capacity), in_specs=[SME...  6.59 us
  transfers between devices with their start and end apart: 4, of which 2 were waited for; matrix products, arithmetic and copies ran while one was open for 2% of the time, Pallas kernels for 37%

profile of v1, /device:TPU:1, one launch (start us, length us, event | category | flops | bytes accessed | tf_op | source)
XLA Modules:
  0.0 104.5 jit_solution(4056382185315511299)
XLA Ops:
  0.6 0.0 copy-start
  0.6 6.4 %shard_map.184 = bf16[8192,128]{1,0:T(8,128)(2,1)} custom-call(s32[64,128]{1,0:T(8,128)} %bitcast.16, bf16[2048,128]{1,0:T(8,128)(2,1)} %nodes_ref.13), custom_call_target="tpu_custom_call" | custom-call | flops 4294967296 | bytes 2097152 | tf_op jit(solution)/shard_map/pallas_call | solution.py:170
  7.1 0.0 copy-start.13
  7.1 0.0 copy-start.10
  7.1 11.5 %all-to-all-start = ((bf16[128,64,128]{2,1,0:T(8,128)(2,1)}), bf16[128,64,128]{2,1,0:T(8,128)(2,1)S(1)}, u32[]{:S(2)}, u32[]{:S(2)}) async-start(bf16[128,64,128]{2,1,0:T(8,128)(2,1)} %bitcast.14), calls=%async_computation | async-start | bytes 4194304 | tf_op jit(solution)/shard_map/all_to_all | solution.py:611
  18.6 0.0 copy-done.13
  18.6 0.6 reshape.40.rows_ref
  19.2 2.2 %shard_map.186 = (bf16[256,128]{1,0:T(8,128)(2,1)}, bf16[256,128]{1,0:T(8,128)(2,1)}) custom-call(s32[4,128]{1,0:T(4,128)} %reshape.40.rows_ref, bf16[2048,128]{1,0:T(8,128)(2,1)} %nodes_ref.13), custom_call_target="tpu_custom_call" | custom-call | flops 268435456 | bytes 655360 | tf_op jit(solution)/shard_map/pallas_call | solution.py:200
  21.4 3.0 %collective-permute-start.1 = (bf16[256,128]{1,0:T(8,128)(2,1)}, bf16[256,128]{1,0:T(8,128)(2,1)S(1)}, u32[]{:S(2)}, u32[]{:S(2)}) collective-permute-start(bf16[256,128]{1,0:T(8,128)(2,1)} %get-tuple-element.14.after_ref), channel_id=1, source_target_pairs={{1,0},{2,1},{3,2},{4,3},{5,4},{6,5},{7,6},{8,7},{9,8},{10,9},{11,1... | collective-permute-start | bytes 196616 | tf_op jit(solution)/shard_map/ppermute | solution.py:616
  24.4 2.8 %collective-permute-start = (bf16[256,128]{1,0:T(8,128)(2,1)}, bf16[256,128]{1,0:T(8,128)(2,1)S(1)}, u32[]{:S(2)}, u32[]{:S(2)}) collective-permute-start(bf16[256,128]{1,0:T(8,128)(2,1)} %get-tuple-element.13), channel_id=1, source_target_pairs={{0,1},{1,2},{2,3},{3,4},{4,5},{5,6},{6,7},{7,8},{8,9},{9,10},{10,1... | collective-permute-start | bytes 196616 | tf_op jit(solution)/shard_map/ppermute | solution.py:615
  27.1 0.0 copy-done.10
  27.2 0.6 reshape.41.source_ref
  27.8 8.2 %shard_map.185.part_hbm = f32[8192,128]{1,0:T(8,128)} custom-call(s32[64,128]{1,0:T(8,128)} %bitcast.15, bf16[2048,128]{1,0:T(8,128)(2,1)} %nodes_ref.13, bf16[8192,128]{1,0:T(8,128)(2,1)} %bitcast.11, bf16[384,128]{1,0:T(8,128)(2,1)} %first_ref.7), custom_call_target="tpu_custom_call" | custom-call | flops 4831838208 | bytes 8388608 | tf_op jit(solution)/shard_map/pallas_call | solution.py:232
  36.0 0.0 copy-start.3
  36.0 0.0 copy-start.6
  36.1 0.0 copy-start.7
  36.1 9.4 %shard_map.187 = (bf16[12288,128]{1,0:T(8,128)(2,1)}, bf16[1024,128]{1,0:T(8,128)(2,1)}, bf16[16,128]{1,0:T(8,128)(2,1)}) custom-call(s32[16,6,128]{2,1,0:T(8,128)} %reshape.41.source_ref, bf16[12288,128]{1,0:T(8,128)(2,1)} %edges_ref.3, bf16[2048,128]{1,0:T(8,128)(2,1)} %nodes_ref.13, bf16[384,128]{1,0:T(8,128)(2,1)} %first_ref.8, ...), custom_call_target="tpu_custom_call" | custom-call | flops 2831155200 | bytes 3145728 | tf_op jit(solution)/shard_map/pallas_call | solution.py:572
  45.5 0.0 copy-done
  45.5 0.2 dynamic-slice_reduce_fusion.counts_ref
  45.7 0.0 copy-start.9
  45.7 0.0 collective-permute-done.1.upper_ref
  45.7 0.0 copy-start.4
  45.7 0.0 collective-permute-done.lower_ref
  45.7 0.0 copy-start.5
  45.7 3.2 %all-to-all-done = bf16[128,64,128]{2,1,0:T(8,128)(2,1)S(1)} async-done(((bf16[128,64,128]{2,1,0:T(8,128)(2,1)}), bf16[128,64,128]{2,1,0:T(8,128)(2,1)S(1)}, u32[]{:S(2)}, u32[]{:S(2)}) %all-to-all-start) | async-done | bytes 2097184 | tf_op jit(solution)/shard_map/all_to_all | solution.py:611
  48.9 0.0 copy-done.3
  49.0 0.0 copy-done.6
  49.0 0.0 copy-done.7
  49.0 0.0 copy-start.8
  49.0 0.7 copy-done.8
  49.6 6.6 %shard_map.188.after_ref.values_ref = bf16[8192,128]{1,0:T(8,128)(2,1)S(1)} custom-call(s32[128]{0:T(128)S(1)} %dynamic-slice_reduce_fusion.counts_ref, bf16[8192,128]{1,0:T(8,128)(2,1)S(1)} %bitcast.8, f32[8192,128]{1,0:T(8,128)} %shard_map.185.part_hbm, bf16[8192,128]{1,0:T(8,128)(2,1)} %bitcast.12, bf16[384,128]{1,0:T(8,128)(2,1)S(1)} %copy-done.3, ...), custom_call_target="tpu_custom_call" | custom-call | flops 1073741824 | bytes 14680064 | tf_op jit(solution)/shard_map/pallas_call | solution.py:303
  56.2 0.0 copy-done.9
  56.2 0.0 copy-done.4
  56.3 0.0 copy-done.5
  56.3 0.0 copy-start.1
  56.3 1.4 %copy-done.1 = bf16[8192,128]{1,0:T(8,128)(2,1)} copy-done((bf16[8192,128]{1,0:T(8,128)(2,1)}, bf16[8192,128]{1,0:T(8,128)(2,1)S(1)}, u32[]{:S(2)}) %copy-start.1) | copy-done | bytes 2097176
  57.7 8.2 %all-to-all-start.1 = ((bf16[128,64,128]{2,1,0:T(8,128)(2,1)}), bf16[128,64,128]{2,1,0:T(8,128)(2,1)S(1)}, u32[]{:S(2)}, u32[]{:S(2)}) async-start(bf16[128,64,128]{2,1,0:T(8,128)(2,1)} %bitcast.9), calls=%async_computation.1 | async-start | bytes 4194304 | tf_op jit(solution)/shard_map/all_to_all | solution.py:639
  65.8 0.0 copy-done.11
  65.8 0.1 copy.24
  65.9 0.1 copy.23
  66.0 0.7 reshape.44.rows_ref
  66.7 0.1 reshape.36.rows_ref
  66.8 9.4 %shard_map.189 = (bf16[12288,128]{1,0:T(8,128)(2,1)}, bf16[1024,128]{1,0:T(8,128)(2,1)}) custom-call(s32[16,6,128]{2,1,0:T(8,128)} %reshape.41.source_ref, bf16[12288,128]{1,0:T(8,128)(2,1)} %edges_ref.3, bf16[2048,128]{1,0:T(8,128)(2,1)} %nodes_ref.13, bf16[384,128]{1,0:T(8,128)(2,1)} %first_ref.8, ...), custom_call_target="tpu_custom_call", output_to_operand_aliasing={{0}: (9, {})} | custom-call | flops 2831155200 | bytes 3145728 | tf_op jit(solution)/shard_map/pallas_call | solution.py:572
  76.2 0.0 copy-start.2
  76.2 9.4 %shard_map.190 = (f32[12288,256]{1,0:T(8,128)}, bf16[96,256,256]{2,1,0:T(8,128)(2,1)}, bf16[8192,128]{1,0:T(8,128)(2,1)}) custom-call(s32[128]{0:T(128)} %copy-done.9, bf16[8192,128]{1,0:T(8,128)(2,1)} %bitcast.13, s32[64,128]{1,0:T(8,128)} %reshape.44.rows_ref, bf16[8192,128]{1,0:T(8,128)(2,1)} %copy-done.1, bf16[2048,128]{1,0:T(8,128)(2,1)} %nodes_ref.13, ...), custom_call_target="tpu_custom_call" | custom-call | flops 4294967296 | bytes 2097152 | tf_op jit(solution)/shard_map/pallas_call | solution.py:407
  85.7 10.7 %all-to-all-done.1 = bf16[128,64,128]{2,1,0:T(8,128)(2,1)S(1)} async-done(((bf16[128,64,128]{2,1,0:T(8,128)(2,1)}), bf16[128,64,128]{2,1,0:T(8,128)(2,1)S(1)}, u32[]{:S(2)}, u32[]{:S(2)}) %all-to-all-start.1) | async-done | bytes 2097184 | tf_op jit(solution)/shard_map/all_to_all | solution.py:639
  96.3 0.0 copy-done.2
  96.3 8.0 %shard_map.191 = bf16[2048,128]{1,0:T(8,128)(2,1)} custom-call(s32[64,128]{1,0:T(8,128)S(1)} %reshape.36.rows_ref, bf16[8192,128]{1,0:T(8,128)(2,1)S(1)} %bitcast.10, f32[12288,256]{1,0:T(8,128)} %get-tuple-element.19.sums_hbm, bf16[96,256,256]{2,1,0:T(8,128)(2,1)} %get-tuple-element.20.prepared_hbm, bf16[2048,128]{1,0:T(8,128)(2,1)S(1)} %copy-done.2), custom_call_target="tpu_custom_call" | custom-call | flops 4294967296 | bytes 4194304 | tf_op jit(solution)/shard_map/pallas_call | solution.py:463
  (3 shorter events, 0.0 us)
Async XLA Ops:
  0.6 44.9 %copy-start = (s32[128,128]{1,0:T(8,128)S(1)}, s32[128,128]{1,0:T(8,128)}, u32[]{:S(2)}) copy-start(s32[128,128]{1,0:T(8,128)} %param.24) | copy-start | bytes 196612
  7.1 11.5 %copy-start.13 = (s32[2,256]{1,0:T(2,128)S(1)}, s32[2,256]{1,0:T(2,128)}, u32[]{:S(2)}) copy-start(s32[2,256]{1,0:T(2,128)} %param.21) | copy-start | bytes 6148
  7.1 20.1 %copy-start.10 = (s32[12288]{0:T(1024)S(1)}, s32[12288]{0:T(1024)}, u32[]{:S(2)}) copy-start(s32[12288]{0:T(1024)} %param.20) | copy-start | bytes 147460
  7.1 41.9 %all-to-all-start = ((bf16[128,64,128]{2,1,0:T(8,128)(2,1)}), bf16[128,64,128]{2,1,0:T(8,128)(2,1)S(1)}, u32[]{:S(2)}, u32[]{:S(2)}) async-start(bf16[128,64,128]{2,1,0:T(8,128)(2,1)} %bitcast.14), calls=%async_computation | async-start | bytes 4194304 | tf_op jit(solution)/shard_map/all_to_all | solution.py:611
  21.4 24.3 %collective-permute-start.1 = (bf16[256,128]{1,0:T(8,128)(2,1)}, bf16[256,128]{1,0:T(8,128)(2,1)S(1)}, u32[]{:S(2)}, u32[]{:S(2)}) collective-permute-start(bf16[256,128]{1,0:T(8,128)(2,1)} %get-tuple-element.14.after_ref), channel_id=1, source_target_pairs={{1,0},{2,1},{3,2},{4,3},{5,4},{6,5},{7,6},{8,7},{9,8},{10,9},{11,1... | collective-permute-start | bytes 196616 | tf_op jit(solution)/shard_map/ppermute | solution.py:616
  24.4 21.3 %collective-permute-start = (bf16[256,128]{1,0:T(8,128)(2,1)}, bf16[256,128]{1,0:T(8,128)(2,1)S(1)}, u32[]{:S(2)}, u32[]{:S(2)}) collective-permute-start(bf16[256,128]{1,0:T(8,128)(2,1)} %get-tuple-element.13), channel_id=1, source_target_pairs={{0,1},{1,2},{2,3},{3,4},{4,5},{5,6},{6,7},{7,8},{8,9},{9,10},{10,1... | collective-permute-start | bytes 196616 | tf_op jit(solution)/shard_map/ppermute | solution.py:615
  36.0 12.9 %copy-start.3 = (bf16[384,128]{1,0:T(8,128)(2,1)S(1)}, bf16[384,128]{1,0:T(8,128)(2,1)}, u32[]{:S(2)}) copy-start(bf16[384,128]{1,0:T(8,128)(2,1)} %first_ref.7) | copy-start | bytes 294916
  36.0 12.9 %copy-start.6 = (bf16[128,128]{1,0:T(8,128)(2,1)S(1)}, bf16[128,128]{1,0:T(8,128)(2,1)}, u32[]{:S(2)}) copy-start(bf16[128,128]{1,0:T(8,128)(2,1)} %second_ref.5) | copy-start | bytes 98308
  36.1 12.9 %copy-start.7 = (bf16[128,128]{1,0:T(8,128)(2,1)S(1)}, bf16[128,128]{1,0:T(8,128)(2,1)}, u32[]{:S(2)}) copy-start(bf16[128,128]{1,0:T(8,128)(2,1)} %third_ref.5) | copy-start | bytes 98308
  45.7 10.6 %copy-start.9 = (s32[128]{0:T(128)}, s32[128]{0:T(128)S(1)}, u32[]{:S(2)}) copy-start(s32[128]{0:T(128)S(1)} %dynamic-slice_reduce_fusion.counts_ref) | copy-start | bytes 1540
  45.7 10.6 %copy-start.4 = (bf16[256,128]{1,0:T(8,128)(2,1)}, bf16[256,128]{1,0:T(8,128)(2,1)S(1)}, u32[]{:S(2)}) copy-start(bf16[256,128]{1,0:T(8,128)(2,1)S(1)} %collective-permute-done.1.upper_ref) | copy-start | bytes 196612
  45.7 10.5 %copy-start.5 = (bf16[256,128]{1,0:T(8,128)(2,1)}, bf16[256,128]{1,0:T(8,128)(2,1)S(1)}, u32[]{:S(2)}) copy-start(bf16[256,128]{1,0:T(8,128)(2,1)S(1)} %collective-permute-done.lower_ref) | copy-start | bytes 196612
  49.0 0.7 copy-start.8
  56.3 1.4 %copy-start.1 = (bf16[8192,128]{1,0:T(8,128)(2,1)}, bf16[8192,128]{1,0:T(8,128)(2,1)S(1)}, u32[]{:S(2)}) copy-start(bf16[8192,128]{1,0:T(8,128)(2,1)S(1)} %shard_map.188.after_ref.values_ref) | copy-start | bytes 6291460
  57.7 8.2 %copy-start.11 = (s32[128,64]{0,1:T(8,128)S(1)}, s32[128,64]{0,1:T(8,128)}, u32[]{:S(2)}) copy-start(s32[128,64]{0,1:T(8,128)} %param.23) | copy-start | bytes 98308
  57.7 8.3 %copy-start.12 = (s32[128,64]{0,1:T(8,128)S(1)}, s32[128,64]{0,1:T(8,128)}, u32[]{:S(2)}) copy-start(s32[128,64]{0,1:T(8,128)} %param.22) | copy-start | bytes 98308
  57.7 38.7 %all-to-all-start.1 = ((bf16[128,64,128]{2,1,0:T(8,128)(2,1)}), bf16[128,64,128]{2,1,0:T(8,128)(2,1)S(1)}, u32[]{:S(2)}, u32[]{:S(2)}) async-start(bf16[128,64,128]{2,1,0:T(8,128)(2,1)} %bitcast.9), calls=%async_computation.1 | async-start | bytes 4194304 | tf_op jit(solution)/shard_map/all_to_all | solution.py:639
  76.2 20.1 %copy-start.2 = (bf16[2048,128]{1,0:T(8,128)(2,1)S(1)}, bf16[2048,128]{1,0:T(8,128)(2,1)}, u32[]{:S(2)}) copy-start(bf16[2048,128]{1,0:T(8,128)(2,1)} %nodes_ref.13) | copy-start | bytes 1572868
